TPU v7x, 512 devices: a whole 4x8x8 slice. The times are simulated.
512 devices in a mesh: group: 16 (over x_lo, z), dev: 32 (over x_hi, y, core).
Axes of the slice: x: 4 (x_hi: 2, x_lo: 2; x = x_hi * 2 + x_lo), y: 8, z: 8, core: 2. Of those that a mesh axis runs over, the one named last changes fastest.
Arguments:
- patches: bfloat16 [16, 32, 256, 1152], P('group', 'dev'), may hold values from -6 to 6
- norm_gain: float32 [1152], replicated, may hold values from 0.1 to 1.9
- kv_weight: bfloat16 [4096, 1152], P(('group', 'dev')), may hold values from -0.1875 to 0.1875
- latent_q: bfloat16 [64, 2048], replicated
- clip_frames: int32 [16, 32], P('group', 'dev'), may hold values from 1 to 8, as said below
- row_owner: int32 [16, 32, 256], P('group', 'dev'), may hold values from 0 to 31, as said below
- row_slot: int32 [16, 32, 256], P('group', 'dev'), may hold values from 0 to 15, as said below
- slot_pos: int32 [16, 32, 512], P('group', 'dev'), may hold values from 0 to 512, as said below
- latent_blocks: int32 [16, 32, 64, 2], P('group', 'dev'), may hold values from -1 to 3, as said below
Outputs:
- latent_out: bfloat16 [2048, 32768], P('dev', 'group')
Inputs may be any that keep to these rules, and one draw needn't show every extreme that they name: `clip_frames`: A group's clips hold 4 * 32 frames together; every group has a clip of 8 frames and one of 2 frames or fewer. `row_owner`: A device holds exactly f * 2 rows of each clip of its group that has f frames. `row_slot`: the rows that one device holds for one clip carry the slots 0, 1, and so on, each once. `slot_pos`: for a clip of f frames the entries s * 16 + k, with k below the number of rows of that clip on device s, name the positions 0 to f * 64 - 1 each once; every other entry is 512. `latent_blocks`: for a clip of b = ceil(f / 2) blocks, entry 0 of latent i is block i * b // 64; entry 1 is a block beside it, or -1 where b is 1.
All inputs are finite; a program needn't handle non-finite values.
Results may differ from a plain program's by a relative error of at most 0.0055.
The roundings to bfloat16 on the way count: a program that leaves them out, or rounds other values in their place, can miss the bound.
Values may be sent and summed in bfloat16 or wider, within the bound.
A program may use at most 64 MiB of HBM per device.

v0:
```python
import jax
import jax.numpy as jnp
from jax import lax
from jax.sharding import PartitionSpec as P

HD = 128
LAT = 64
FR_ROWS = 64


def rms_rows(patch_rows, norm_gain):
    widened = patch_rows.astype(jnp.float32)
    inverse_rms = lax.rsqrt(jnp.mean(widened * widened, axis=-1, keepdims=True) + 1e-06)
    return (widened * inverse_rms * norm_gain).astype(jnp.bfloat16)


def product_rows(input_rows, weight_piece):
    return lax.dot_general(
        input_rows, weight_piece, (((1,), (1,)), ((), ())), preferred_element_type=jnp.float32
    )


def project(input_rows, kv_weight, live_rows):
    block_rows = 2 * FR_ROWS
    block_count = input_rows.shape[0] // block_rows
    weight_piece = lax.all_gather(kv_weight, ("group", "dev"), axis=0, tiled=True)
    outputs = []
    for block in range(block_count):
        rows_here = input_rows[block * block_rows : (block + 1) * block_rows]
        empty = jnp.zeros((block_rows, weight_piece.shape[0]), jnp.float32)
        outputs.append(
            lax.cond(
                block * block_rows < live_rows,
                lambda: product_rows(rows_here, weight_piece),
                lambda: empty,
            )
        )
    projected = jnp.concatenate(outputs, axis=0)
    return projected.astype(jnp.bfloat16)


def attend(keyval, frames, listed, latent_q):
    capacity = keyval.shape[0]
    kv_width = keyval.shape[1] // 2
    head_count = kv_width // HD
    key_part = keyval[:, :kv_width].reshape(capacity, head_count, HD)
    value_part = keyval[:, kv_width:].reshape(capacity, head_count, HD)
    queries = latent_q.reshape(LAT, head_count, HD)
    scores = jnp.einsum(
        "ihd,jhd->hij", queries, key_part, preferred_element_type=jnp.float32
    ) * HD ** (-0.5)
    position = jnp.arange(capacity, dtype=jnp.int32)
    block_id = position // (2 * FR_ROWS)
    allowed = ((block_id[None, :] == listed[:, 0:1]) | (block_id[None, :] == listed[:, 1:2])) & (
        position[None, :] < frames * FR_ROWS
    )
    scores = jnp.where(allowed[None, :, :], scores, jnp.float32(-1e30))
    row_max = jnp.max(scores, axis=-1, keepdims=True)
    raised = jnp.exp(scores - row_max)
    row_sum = jnp.sum(raised, axis=-1, keepdims=True)
    attn_weights = (raised / row_sum).astype(jnp.bfloat16)
    blended = jnp.einsum(
        "hij,jhd->hdi", attn_weights, value_part, preferred_element_type=jnp.float32
    )
    return blended.astype(jnp.bfloat16).reshape(kv_width, LAT)


def per_device(
    patches,
    norm_gain,
    kv_weight,
    latent_q,
    clip_frames,
    row_owner,
    row_slot,
    slot_pos,
    latent_blocks,
):
    dev_count = lax.axis_size("dev")
    normed = rms_rows(patches[0, 0], norm_gain)
    places = slot_pos[0, 0]
    capacity = places.shape[0]
    slot_count = capacity // dev_count
    target = row_owner[0, 0] * slot_count + row_slot[0, 0]
    frames = clip_frames[0, 0]
    outbox = jnp.zeros((capacity, normed.shape[1]), jnp.bfloat16).at[target].set(normed)
    received = lax.all_to_all(
        outbox.reshape(dev_count, slot_count, normed.shape[1]),
        "dev",
        split_axis=0,
        concat_axis=0,
        tiled=True,
    )
    timeline = (
        jnp.zeros_like(outbox)
        .at[places]
        .set(received.reshape(capacity, normed.shape[1]), mode="drop")
    )
    keyval = project(timeline, kv_weight, frames * FR_ROWS)
    blended = attend(keyval, frames, latent_blocks[0, 0], latent_q)
    return lax.all_to_all(blended, "dev", split_axis=0, concat_axis=1, tiled=True)


def solution(mesh):
    return jax.shard_map(
        per_device,
        mesh=mesh,
        in_specs=(
            P("group", "dev", None, None),
            P(),
            P(("group", "dev"), None),
            P(),
            P("group", "dev"),
            P("group", "dev", None),
            P("group", "dev", None),
            P("group", "dev", None),
            P("group", "dev", None, None),
        ),
        out_specs=P("dev", "group"),
        check_vma=False,
    )
```

profile of v0, /device:TPU:1, one launch (start us, length us, event | category | flops | bytes accessed | tf_op | source)
XLA Modules:
  0.0 911.5 jit_solution(12294368740215103621)
XLA Ops:
  6.5 0.7 all-gather.2.cloned.1.call-update
  7.3 1.3 fusion.10
  8.6 0.7 compare_select_fusion.1
  9.3 3.3 scatter_custom_fusion
  12.6 11.2 %all-to-all-start = ((bf16[32,16,1152]{2,1,0:T(8,128)(2,1)}), bf16[32,16,1152]{2,1,0:T(8,128)(2,1)S(1)}, u32[]{:S(2)}, u32[]{:S(2)}) async-start(bf16[32,16,1152]{2,1,0:T(8,128)(2,1)} %bitcast.7), calls=%async_computation | async-start | bytes 2359296 | tf_op jit(solution)/shard_map/all_to_all | solution.py:87
  24.5 0.7 or_and_fusion
  25.3 29.3 %all-to-all-done = bf16[32,16,1152]{2,1,0:T(8,128)(2,1)S(1)} async-done(((bf16[32,16,1152]{2,1,0:T(8,128)(2,1)}), bf16[32,16,1152]{2,1,0:T(8,128)(2,1)S(1)}, u32[]{:S(2)}, u32[]{:S(2)}) %all-to-all-start) | async-done | bytes 1179680 | tf_op jit(solution)/shard_map/all_to_all | solution.py:87
  54.6 3.1 scatter_custom_fusion.1
  57.7 779.5 %all-gather.2.cloned.1.call-done = bf16[4096,1152]{1,0:T(8,128)(2,1)} async-done(((bf16[8,1152]{1,0:T(8,128)(2,1)}), bf16[4096,1152]{1,0:T(8,128)(2,1)}) %all-gather.2.cloned.1.call-update) | async-done | bytes 9437200 | tf_op jit(solution)/shard_map/all_gather | solution.py:26
  837.2 6.8 conditional.4
  837.2 6.8 fusion
  844.0 0.7 copy.28
  844.7 0.1 conditional.5
  844.7 0.1 broadcast.143
  844.8 1.3 copy.29
  846.1 0.1 conditional.6
  846.2 1.3 copy.30
  847.5 0.3 conditional.7
  847.8 1.3 copy.31
  849.1 1.8 pad_maximum_fusion
  850.9 1.6 fusion.37
  852.5 0.4 fusion.24
  853.0 0.3 copy-done.2
  853.3 0.7 fusion.38
  854.0 3.5 convolution_convert_fusion
  857.5 0.2 copy.35
  857.7 0.2 all_to_all.18
  857.9 0.2 copy.47
  858.1 0.4 reshape.211
  858.5 44.8 %all_to_all.24 = bf16[32,2,2048]{2,1,0:T(2,128)(2,1)S(1)} all-to-all(bf16[32,2,2048]{2,1,0:T(2,128)(2,1)S(1)} %reshape.211), channel_id=1, replica_groups=mesh['group'=16,'dev'=32] {'dev'}, dimensions={0} | all-to-all | bytes 524288 | tf_op jit(solution)/shard_map/all_to_all | solution.py:101
  903.3 0.4 reshape.212
  903.7 0.9 copy.40
  (17 shorter events, 0.2 us)
Async XLA Ops:
  6.5 846.0 %copy-start = (bf16[64,2048]{1,0:T(8,128)(2,1)S(1)}, bf16[64,2048]{1,0:T(8,128)(2,1)}, u32[]{:S(2)}) copy-start(bf16[64,2048]{1,0:T(8,128)(2,1)} %param.20) | copy-start | bytes 786436
  6.5 830.7 %all-gather.2.cloned.1.call-start = ((), (), s32[]{:S(2)}) async-start(), calls=%async_computation.2 | async-start | bytes 9455616 | tf_op jit(solution)/shard_map/all_gather | solution.py:26
  8.5 16.0 %copy-start.4 = (s32[1,1,64,2]{2,3,1,0:T(2,128)S(1)}, s32[1,1,64,2]{2,3,1,0:T(2,128)}, u32[]{:S(2)}) copy-start(s32[1,1,64,2]{2,3,1,0:T(2,128)} %param.25) | copy-start | bytes 1540
  8.5 16.0 %copy-start.3 = (s32[1,1,512]{2,1,0:T(1,128)S(1)}, s32[1,1,512]{2,1,0:T(1,128)}, u32[]{:S(2)}) copy-start(s32[1,1,512]{2,1,0:T(1,128)} %param.24) | copy-start | bytes 6148
  12.6 42.0 %all-to-all-start = ((bf16[32,16,1152]{2,1,0:T(8,128)(2,1)}), bf16[32,16,1152]{2,1,0:T(8,128)(2,1)S(1)}, u32[]{:S(2)}, u32[]{:S(2)}) async-start(bf16[32,16,1152]{2,1,0:T(8,128)(2,1)} %bitcast.7), calls=%async_computation | async-start | bytes 2359296 | tf_op jit(solution)/shard_map/all_to_all | solution.py:87
  847.8 1.3 copy-start.1
  852.5 0.8 copy-start.2
Sparse Core Ops, SparseCore 0:
  9.6 827.5 all-gather.1
where the time goes:
time: 912 us; the launch traced here: 911 us
  waiting for transfers between devices  810 us (89%)
  blocking collectives  44.8 us (5%)
  between operations  14.2 us (2%)
  local copies, waits for them, and re-layouts  12.1 us (1%)
  starting transfers between devices  11.2 us (1%)
  matrix products  10.7 us (1%)
    all_gather x1, waiting for transfers between devices, project(): lax.all_gather(kv_weight, ('group', 'dev'), axis=0, tiled=True)  780 us
    all_to_all x1, blocking collectives, per_device(): lax.all_to_all(blended, 'dev', split_axis=0, concat_axis=1, tiled=True)  44.8 us
    all_to_all x1, waiting for transfers between devices, per_device(): lax.all_to_all(outbox.reshape(dev_count, slot_count, normed.shape[1]), 'd...  29.3 us
  transfers between devices with their start and end apart: 2, of which 2 were waited for; matrix products, arithmetic and copies ran while one was open for 1% of the time, Pallas kernels for 0%

commit v1 on v0

--- a/solution.py
+++ b/solution.py
@@ -23,7 +23,12 @@
 def project(input_rows, kv_weight, live_rows):
     block_rows = 2 * FR_ROWS
     block_count = input_rows.shape[0] // block_rows
-    weight_piece = lax.all_gather(kv_weight, ("group", "dev"), axis=0, tiled=True)
+    weight_piece = jnp.concatenate(
+        lax.all_to_all(
+            jnp.stack([kv_weight] * lax.axis_size(("group", "dev"))), ("group", "dev"), 0, 0
+        ),
+        axis=0,
+    )
     outputs = []
     for block in range(block_count):
         rows_here = input_rows[block * block_rows : (block + 1) * block_rows]

time: 912 us -> 344 us (0.38)
  waiting for transfers between devices: 810 us -> 205 us
  blocking collectives: 44.8 us -> 85.8 us
  between operations: 14.2 us -> 0.85 us
    all_gather x1 -> x0, waiting for transfers between devices: 780 us -> none  [project(): lax.all_gather(kv_weight, ('group', 'dev'), axis=0, tiled=True)]
    all_to_all x1, waiting for transfers between devices: 29.3 us -> 205 us  [project(): lax.all_to_all(jnp.stack([kv_weight] * lax.axis_size(('group', 'dev'))),...]
    all_to_all x0 -> x1, blocking collectives: none -> 44.1 us  [per_device(): lax.all_to_all(outbox.reshape(dev_count, slot_count, normed.shape[1]), 'd...]
  transfers between devices with their start and end apart: 2 -> 1, of which waited for: 2 -> 1; matrix products, arithmetic and copies ran while one was open for 1% -> 1% of each run, Pallas kernels for 0% -> 0%
where the time goes in v1:
time: 344 us; the launch traced here: 343 us
  waiting for transfers between devices  205 us (60%)
  blocking collectives  85.8 us (25%)
  local copies, waits for them, and re-layouts  16.5 us (5%)
  starting transfers between devices  16.5 us (5%)
  matrix products  10.7 us (3%)
  other arithmetic  7.81 us (2%)
    all_to_all x1, waiting for transfers between devices, project(): lax.all_to_all(jnp.stack([kv_weight] * lax.axis_size(('group', 'dev'))),...  205 us
    all_to_all x1, blocking collectives, per_device(): lax.all_to_all(outbox.reshape(dev_count, slot_count, normed.shape[1]), 'd...  44.1 us
    all_to_all x1, blocking collectives, per_device(): lax.all_to_all(blended, 'dev', split_axis=0, concat_axis=1, tiled=True)  41.7 us
    all_to_all x1, starting transfers between devices, project(): lax.all_to_all(jnp.stack([kv_weight] * lax.axis_size(('group', 'dev'))),...  16.5 us
  transfers between devices with their start and end apart: 1, of which 1 were waited for; matrix products, arithmetic and copies ran while one was open for 1% of the time, Pallas kernels for 0%

profile of v1, /device:TPU:1, one launch (start us, length us, event | category | flops | bytes accessed | tf_op | source)
XLA Modules:
  0.0 342.9 jit_solution(15000831957269959481)
XLA Ops:
  0.0 1.3 fusion.10
  1.3 0.7 compare_select_fusion.1
  2.0 2.6 scatter_custom_fusion
  4.6 44.1 %all_to_all.29 = bf16[32,16,1152]{2,1,0:T(8,128)(2,1)S(1)} all-to-all(bf16[32,16,1152]{2,1,0:T(8,128)(2,1)S(1)} %bitcast.58), channel_id=1, replica_groups=mesh['group'=16,'dev'=32] {'dev'}, dimensions={0} | all-to-all | bytes 2359296 | tf_op jit(solution)/shard_map/all_to_all | solution.py:92
  48.7 4.3 %stack.2 = bf16[512,8,1152]{2,1,0:T(8,128)(2,1)} broadcast(bf16[8,1152]{1,0:T(8,128)(2,1)S(1)} %copy-done.3), dimensions={1,2} | broadcast | bytes 9455616 | tf_op jit(solution)/shard_map/stack | solution.py:28
  53.1 16.5 %all-to-all-start.1 = ((bf16[512,8,1152]{2,1,0:T(8,128)(2,1)}), bf16[512,8,1152]{2,1,0:T(8,128)(2,1)}, u32[]{:S(2)}, u32[]{:S(2)}) async-start(bf16[512,8,1152]{2,1,0:T(8,128)(2,1)} %stack.2), calls=%async_computation.1 | async-start | bytes 18874368 | tf_op jit(solution)/shard_map/all_to_all | solution.py:27
  70.3 0.7 or_and_fusion
  71.0 3.1 scatter_custom_fusion.1
  74.1 204.6 %all-to-all-done.1 = bf16[512,8,1152]{2,1,0:T(8,128)(2,1)} async-done(((bf16[512,8,1152]{2,1,0:T(8,128)(2,1)}), bf16[512,8,1152]{2,1,0:T(8,128)(2,1)}, u32[]{:S(2)}, u32[]{:S(2)}) %all-to-all-start.1) | async-done | bytes 9437216 | tf_op jit(solution)/shard_map/all_to_all | solution.py:27
  278.6 6.8 %conditional.4 = (bf16[128,4096]{1,0:T(8,128)(2,1)S(1)}) conditional(s32[]{:T(128)} %convert_element_type.28, () %tuple.29, (bf16[512,1152]{1,0:T(8,128)(2,1)S(1)}, bf16[4096,1152]{1,0:T(8,128)(2,1)}) %tuple.30), branch_computations={%region_3.0_spmd, %region_4.0_spmd} | conditional | flops 1207959552 | bytes 10780680 | solution.py:37
  278.6 6.8 %fusion = bf16[128,4096]{1,0:T(8,128)(2,1)S(1)} fusion(bf16[4096,1152]{1,0:T(8,128)(2,1)} %get-tuple-element.38, bf16[512,1152]{1,0:T(8,128)(2,1)S(1)} %get-tuple-element.37), kind=kOutput, calls=%fused_computation.2 | convolution fusion | flops 1207959552 | bytes 10780672 | tf_op jit(solution)/shard_map/cond/branch_1_fun/dot_general | solution.py:18
  285.4 0.7 copy.28
  286.1 0.3 conditional.5
  286.1 0.1 broadcast.145
  286.4 1.3 copy.29
  287.7 0.1 conditional.6
  287.8 1.3 copy.30
  289.1 0.1 conditional.7
  289.3 1.3 copy.31
  290.6 1.8 pad_maximum_fusion
  292.4 1.6 fusion.37
  294.0 0.4 fusion.24
  294.4 0.3 copy-done.2
  294.8 0.7 fusion.38
  295.5 3.5 %convolution_convert_fusion = bf16[16,128,64]{1,2,0:T(8,128)(2,1)S(1)} fusion(bf16[512,16,128]{0,2,1:T(8,128)(2,1)} %bitcast.61, f32[16,64]{1,0:T(8,128)S(1)} %fusion.38, f32[16,512,64]{1,2,0:T(8,128)S(1)} %fusion.24, pred[64,512]{1,0:T(8,128)(4,1)S(1)} %copy-done.2), kind=kOutput, calls=%fused_computation.18 | convolution fusion | flops 136971776 | bytes 4493312 | tf_op jit(solution)/shard_map/hij,jhd->hdi/dot_general | solution.py:67
  299.0 0.2 copy.35
  299.1 0.2 all_to_all.22
  299.4 0.2 copy.47
  299.6 0.4 reshape.217
  300.0 41.7 %all_to_all.30 = bf16[32,2,2048]{2,1,0:T(2,128)(2,1)S(1)} all-to-all(bf16[32,2,2048]{2,1,0:T(2,128)(2,1)S(1)} %reshape.217), channel_id=1, replica_groups=mesh['group'=16,'dev'=32] {'dev'}, dimensions={0} | all-to-all | bytes 524288 | tf_op jit(solution)/shard_map/all_to_all | solution.py:106
  341.7 0.4 reshape.218
  342.0 0.9 copy.40
  (18 shorter events, 0.2 us)
Async XLA Ops:
  0.0 294.0 %copy-start = (bf16[64,2048]{1,0:T(8,128)(2,1)S(1)}, bf16[64,2048]{1,0:T(8,128)(2,1)}, u32[]{:S(2)}) copy-start(bf16[64,2048]{1,0:T(8,128)(2,1)} %param.20) | copy-start | bytes 786436
  1.3 47.4 %copy-start.3 = (bf16[8,1152]{1,0:T(8,128)(2,1)S(1)}, bf16[8,1152]{1,0:T(8,128)(2,1)}, u32[]{:S(2)}) copy-start(bf16[8,1152]{1,0:T(8,128)(2,1)} %param.19) | copy-start | bytes 55300
  53.1 17.2 %copy-start.5 = (s32[1,1,64,2]{2,3,1,0:T(2,128)S(1)}, s32[1,1,64,2]{2,3,1,0:T(2,128)}, u32[]{:S(2)}) copy-start(s32[1,1,64,2]{2,3,1,0:T(2,128)} %param.25) | copy-start | bytes 1540
  53.1 17.2 %copy-start.4 = (s32[1,1,512]{2,1,0:T(1,128)S(1)}, s32[1,1,512]{2,1,0:T(1,128)}, u32[]{:S(2)}) copy-start(s32[1,1,512]{2,1,0:T(1,128)} %param.24) | copy-start | bytes 6148
  53.1 225.6 %all-to-all-start.1 = ((bf16[512,8,1152]{2,1,0:T(8,128)(2,1)}), bf16[512,8,1152]{2,1,0:T(8,128)(2,1)}, u32[]{:S(2)}, u32[]{:S(2)}) async-start(bf16[512,8,1152]{2,1,0:T(8,128)(2,1)} %stack.2), calls=%async_computation.1 | async-start | bytes 18874368 | tf_op jit(solution)/shard_map/all_to_all | solution.py:27
  289.3 1.3 copy-start.1
  294.0 0.8 copy-start.2
